TPU v7x, 256 devices: a whole 4x4x8 slice. The times are simulated.
256 devices in a mesh: batch: 8 (over z), proto: 32 (over y, x, core).
Axes of the slice: x: 4, y: 4, z: 8, core: 2. Of those that a mesh axis runs over, the one named last changes fastest.
Arguments:
- student_features: bfloat16 [12288, 256], P('batch'), may hold values from -8 to 8, as said below
- teacher_features: bfloat16 [12288, 256], P('batch'), may hold values from -8 to 8, as said below
- student_protos: bfloat16 [256, 65536], P(None, 'proto'), may hold values from -2 to 2, as said below
- teacher_protos: bfloat16 [256, 65536], P(None, 'proto'), may hold values from -2 to 2
Outputs:
- feature_grads: float32 [12288, 256], P('batch')
- proto_grads: float32 [65536, 256], P('proto')
Inputs may be any that keep to these rules, and one draw needn't show every extreme that they name: `student_features`: features of one crop; student and teacher features of a crop are related. `teacher_features`: features of one crop. `student_protos`: the teacher prototypes lie near the student ones.
All inputs are finite; a program needn't handle non-finite values.
Results may differ from a plain program's by a relative error of at most 0.0067.
Values sent between devices are 32-bit elements; how exact they have to be, the bound alone decides.
A program may use at most 128 MiB of HBM per device.

v0:
```python
import jax
import jax.numpy as jnp
from jax import lax
from jax.sharding import PartitionSpec as P

ITERS = 3


teacher_temp = 0.04
student_temp = 0.1
loss_scale = 4096.0
epsilon = 1e-06


def unit_rows(values):
    floats = values.astype(jnp.float32)
    length = jnp.sqrt(jnp.sum(floats * floats, axis=1, keepdims=True) + epsilon)
    return (floats / length, length)


def project_back(grads, unit, length):
    return (grads - unit * jnp.sum(unit * grads, axis=1, keepdims=True)) / length


def on_device(student_features, teacher_features, student_protos, teacher_protos):
    student_unit, student_len = unit_rows(student_features)
    teacher_unit, _ = unit_rows(teacher_features)
    proto_unit, proto_len = unit_rows(student_protos.T)
    anchor_unit, _ = unit_rows(teacher_protos.T)
    student_half = student_unit.astype(jnp.bfloat16)
    teacher_half = teacher_unit.astype(jnp.bfloat16)
    proto_half = proto_unit.astype(jnp.bfloat16)
    anchor_half = anchor_unit.astype(jnp.bfloat16)
    contract_last = (((1,), (1,)), ((), ()))
    contract_first = (((0,), (0,)), ((), ()))
    teacher_exp = jnp.exp(
        lax.dot_general(
            teacher_half, anchor_half, contract_last, preferred_element_type=jnp.float32
        )
        / teacher_temp
    )
    student_exp = jnp.exp(
        lax.dot_general(student_half, proto_half, contract_last, preferred_element_type=jnp.float32)
        / student_temp
    )
    student_total = lax.psum(jnp.sum(student_exp, axis=1), "proto")
    predicted = student_exp / student_total[:, None]
    weights = teacher_exp
    for sweep in range(ITERS):
        partial_cols = jnp.sum(weights, axis=0)
        column_total = lax.psum(partial_cols, "batch")
        weights = weights / column_total[None, :]
        partial_rows = jnp.sum(weights, axis=1)
        row_total = lax.psum(partial_rows, "proto")
        weights = weights / row_total[:, None]
    grad_logits = (loss_scale * (predicted - weights) / student_temp).astype(jnp.bfloat16)
    feature_terms = lax.psum(
        jnp.dot(grad_logits, proto_half, preferred_element_type=jnp.float32), "proto"
    )
    feature_grads = project_back(feature_terms, student_unit, student_len)
    proto_local = lax.dot_general(
        grad_logits, student_half, contract_first, preferred_element_type=jnp.float32
    )
    proto_terms = lax.psum(proto_local, "batch")
    proto_grads = project_back(proto_terms, proto_unit, proto_len)
    return (feature_grads, proto_grads)


def solution(mesh):
    return jax.shard_map(
        on_device,
        mesh=mesh,
        in_specs=(P("batch", None), P("batch", None), P(None, "proto"), P(None, "proto")),
        out_specs=(P("batch", None), P("proto", None)),
        check_vma=False,
    )
```

profile of v0, /device:TPU:1, one launch (start us, length us, event | category | flops | bytes accessed | tf_op | source)
XLA Modules:
  0.0 583.5 jit_solution(17540532809071100166)
XLA Ops:
  11.5 1.5 copy.6
  13.4 8.2 %fusion.35 = (f32[2048]{0:T(1024)S(1)}, f32[1536,2048]{1,0:T(8,128)}) fusion(bf16[256,2048]{1,0:T(8,128)(2,1)} %param.7, f32[2048]{0:T(1024)S(1)} %add_sqrt_fusion, bf16[1536,256]{1,0:T(8,128)(2,1)} %param.5, f32[1536]{0:T(1024)S(1)} %add_sqrt_fusion.1), kind=kOutput, calls=%fused_computation.52 | convolution fusion | flops 1619654656 | bytes 14440448 | tf_op jit(solution)/shard_map/dot_general | solution.py:37
  21.6 17.5 %psum.64 = f32[2048]{0:T(1024)S(1)} all-reduce(f32[2048]{0:T(1024)S(1)} %get-tuple-element.4), channel_id=1, replica_groups=mesh['batch'=8,'proto'=32] {'batch'}, use_global_device_ids=true, to_apply=%region_7.0 | all-reduce | flops 2048 | bytes 16384 | tf_op jit(solution)/shard_map/psum | solution.py:51
  39.1 5.5 divide_reduce_fusion
  44.6 67.5 %psum.65 = f32[1536]{0:T(1024)S(1)} all-reduce(f32[1536]{0:T(1024)S(1)} %divide_reduce_fusion), channel_id=1, replica_groups=mesh['batch'=8,'proto'=32] {'proto'}, use_global_device_ids=true, to_apply=%region_9.0 | all-reduce | flops 1536 | bytes 12288 | tf_op jit(solution)/shard_map/psum | solution.py:54
  112.1 5.9 %fusion.9 = f32[2048]{0:T(1024)S(1)} fusion(f32[1536,2048]{1,0:T(8,128)} %get-tuple-element.5, f32[1536]{0:T(1024)S(1)} %psum.65, f32[2048]{0:T(1024)S(1)} %psum.64), kind=kLoop, calls=%fused_computation.14 | loop fusion | flops 9435136 | bytes 12605440 | tf_op jit(solution)/shard_map/reduce_sum | solution.py:50
  118.1 10.9 %psum.66 = f32[2048]{0:T(1024)S(1)} all-reduce(f32[2048]{0:T(1024)S(1)} %fusion.9), channel_id=1, replica_groups=mesh['batch'=8,'proto'=32] {'batch'}, use_global_device_ids=true, to_apply=%region_11.0 | all-reduce | flops 2048 | bytes 16384 | tf_op jit(solution)/shard_map/psum | solution.py:51
  129.0 6.2 %fusion.10 = f32[1536]{0:T(1024)S(1)} fusion(f32[1536,2048]{1,0:T(8,128)} %get-tuple-element.5, f32[2048]{0:T(1024)S(1)} %psum.66, f32[1536]{0:T(1024)S(1)} %psum.65, f32[2048]{0:T(1024)S(1)} %psum.64), kind=kLoop, calls=%fused_computation.15 | loop fusion | flops 12581376 | bytes 12611584 | tf_op jit(solution)/shard_map/reduce_sum | solution.py:53
  135.3 68.0 %psum.67 = f32[1536]{0:T(1024)S(1)} all-reduce(f32[1536]{0:T(1024)S(1)} %fusion.10), channel_id=1, replica_groups=mesh['batch'=8,'proto'=32] {'proto'}, use_global_device_ids=true, to_apply=%region_13.0 | all-reduce | flops 1536 | bytes 12288 | tf_op jit(solution)/shard_map/psum | solution.py:54
  203.2 6.5 %fusion.11 = f32[2048]{0:T(1024)S(1)} fusion(f32[1536,2048]{1,0:T(8,128)} %get-tuple-element.5, f32[1536]{0:T(1024)S(1)} %psum.67, f32[2048]{0:T(1024)S(1)} %psum.66, f32[1536]{0:T(1024)S(1)} %psum.65, f32[2048]{0:T(1024)S(1)} %psum.64), kind=kLoop, calls=%fused_computation.16 | loop fusion | flops 15726592 | bytes 12619776 | tf_op jit(solution)/shard_map/reduce_sum | solution.py:50
  209.7 12.7 %psum.68 = f32[2048]{0:T(1024)S(1)} all-reduce(f32[2048]{0:T(1024)S(1)} %fusion.11), channel_id=1, replica_groups=mesh['batch'=8,'proto'=32] {'batch'}, use_global_device_ids=true, to_apply=%region_15.0 | all-reduce | flops 2048 | bytes 16384 | tf_op jit(solution)/shard_map/psum | solution.py:51
  222.4 6.8 %fusion.12 = f32[1536]{0:T(1024)S(1)} fusion(f32[1536,2048]{1,0:T(8,128)} %get-tuple-element.5, f32[2048]{0:T(1024)S(1)} %psum.68, f32[1536]{0:T(1024)S(1)} %psum.67, f32[2048]{0:T(1024)S(1)} %psum.66, f32[1536]{0:T(1024)S(1)} %psum.65, f32[2048]{0:T(1024)S(1)} %psum.64), kind=kLoop, calls=%fused_computation.17 | loop fusion | flops 18872832 | bytes 12625920 | tf_op jit(solution)/shard_map/reduce_sum | solution.py:53
  229.2 5.9 %fusion.14 = (f32[1536]{0:T(1024)S(1)}, f32[1536,2048]{1,0:T(8,128)}) fusion(f32[2048]{0:T(1024)S(1)} %add_sqrt_fusion.2, bf16[256,2048]{0,1:T(8,128)(2,1)S(1)} %copy.6, f32[1536]{0:T(1024)S(1)} %add_sqrt_fusion.3, bf16[1536,256]{1,0:T(8,128)(2,1)S(1)} %copy-done), kind=kOutput, calls=%fused_computation.19 | convolution fusion | flops 1619655168 | bytes 14438400 | tf_op jit(solution)/shard_map/dot_general | solution.py:43
  235.1 122.8 %all-reduce = (f32[1536]{0:T(1024)S(1)}, f32[1536]{0:T(1024)S(1)}) all-reduce(f32[1536]{0:T(1024)S(1)} %fusion.12, f32[1536]{0:T(1024)S(1)} %get-tuple-element.6), channel_id=1, replica_groups=mesh['batch'=8,'proto'=32] {'proto'}, use_global_device_ids=true, to_apply=%region_17.0 | all-reduce | flops 3072 | bytes 24576 | tf_op jit(solution)/shard_map/psum | solution.py:54
  357.9 11.5 %fusion.13 = bf16[1536,2048]{1,0:T(8,128)(2,1)S(1)} fusion(f32[1536,2048]{1,0:T(8,128)} %get-tuple-element.5, f32[1536,2048]{1,0:T(8,128)} %get-tuple-element.7, f32[1536]{0:T(1024)S(1)} %get-tuple-element.2, f32[2048]{0:T(1024)S(1)} %psum.68, f32[1536]{0:T(1024)S(1)} %psum.67, f32[2048]{0:T(1024)S(1)} %psum.66, f32[1536]{0:T(1024)S(1)} %psum.65, ...), kind=kLoop, calls=%fused_computation.18 | loop fusion | flops 34603008 | bytes 31506432 | tf_op jit(solution)/shard_map/convert_element_type | solution.py:56
  369.4 2.7 copy-done.1
  372.0 3.1 fusion.26
  375.2 6.2 %fusion.30 = f32[2048,256]{1,0:T(8,128)} fusion(bf16[1536,2048]{1,0:T(8,128)(2,1)} %copy-done.1, bf16[1536,256]{1,0:T(8,128)(2,1)S(1)} %copy-done, f32[1536]{0:T(1024)S(1)} %add_sqrt_fusion.3), kind=kOutput, calls=%fused_computation.45 | convolution fusion | flops 1611792384 | bytes 9181184 | tf_op jit(solution)/shard_map/dot_general | solution.py:61
  381.4 108.0 %all-reduce.4.cloned.1.call-done = f32[1536,256]{1,0:T(8,128)} async-done(((f32[1536,256]{1,0:T(8,128)}), f32[1536,256]{1,0:T(8,128)}) %all-reduce.4.cloned.1.call-update) | async-done | bytes 1572880 | tf_op jit(solution)/shard_map/psum | solution.py:57
  489.4 1.9 multiply_reduce_fusion.1
  491.4 3.0 subtract_divide_fusion.1
  494.4 76.8 %all-reduce.6.cloned.1.call-done = f32[2048,256]{1,0:T(8,128)} async-done(((f32[2048,256]{1,0:T(8,128)}), f32[2048,256]{1,0:T(8,128)}) %all-reduce.6.cloned.1.call-update) | async-done | bytes 2097168 | tf_op jit(solution)/shard_map/psum | solution.py:64
  571.2 2.3 multiply_reduce_fusion
  573.5 3.2 subtract_divide_fusion
  (15 shorter events, 4.8 us)
Async XLA Ops:
  7.2 482.3 %all-reduce.4.cloned.1.call-start = ((), (), s32[]{:S(2)}) async-start(), calls=%async_computation | async-start | bytes 3145728 | tf_op jit(solution)/shard_map/psum | solution.py:57
  222.4 6.8 %copy-start = (bf16[1536,256]{1,0:T(8,128)(2,1)S(1)}, bf16[1536,256]{1,0:T(8,128)(2,1)}, u32[]{:S(2)}) copy-start(bf16[1536,256]{1,0:T(8,128)(2,1)} %param.4) | copy-start | bytes 2359300
  369.4 2.7 copy-start.1
  375.1 196.1 %all-reduce.6.cloned.1.call-start = ((), (), s32[]{:S(2)}) async-start(), calls=%async_computation.1 | async-start | bytes 4194304 | tf_op jit(solution)/shard_map/psum | solution.py:64
Sparse Core Ops, SparseCore 0:
  375.3 114.1 all-reduce.3
  492.5 78.6 all-reduce.5
where the time goes:
time: 586 us; the launch traced here: 583 us
  blocking collectives  299 us (51%)
  waiting for transfers between devices  185 us (32%)
  other arithmetic  57.4 us (10%)
  matrix products  23.4 us (4%)
  between operations  14.2 us (2%)
    psum x3, blocking collectives, on_device(): row_total = lax.psum(partial_rows, 'proto')  258 us
    psum x1, waiting for transfers between devices, on_device(): lax.psum(jnp.dot(grad_logits, proto_half, preferred_element_type=jnp.floa...  108 us
    psum x1, waiting for transfers between devices, on_device(): proto_terms = lax.psum(proto_local, 'batch')  76.8 us
    psum x3, blocking collectives, on_device(): column_total = lax.psum(partial_cols, 'batch')  41.1 us
    reduce_sum x3, other arithmetic, on_device(): partial_rows = jnp.sum(weights, axis=1)  18.5 us
    reduce_sum x2, other arithmetic, on_device(): partial_cols = jnp.sum(weights, axis=0)  12.4 us
  transfers between devices with their start and end apart: 2, of which 2 were waited for; matrix products, arithmetic and copies ran while one was open for 2% of the time, Pallas kernels for 0%

commit v1 on v0

v1 whole, which is shorter than its diff:
```python
import jax
import jax.numpy as jnp
from jax import lax
from jax.experimental import pallas as pl
from jax.experimental.pallas import tpu as pltpu
from jax.sharding import PartitionSpec as P

MESH = pl.DeviceIdType.MESH
F32 = jnp.float32
BF16 = jnp.bfloat16

epsilon = 1e-06
teacher_rate = 25.0
student_rate = 10.0
grad_scale = 40960.0

CROPS = 1536
PROTOS = 2048
D = 256
Z = 8
CHIPS = 16
OWN = PROTOS // Z
SUB = OWN // 4
HALF = CROPS // 2
PIECE = HALF // CHIPS


def rows_at(start, size, step):
    return pl.ds(pl.multiple_of(start, step), size)


def normalise_rows(src, dst):
    def body(i, carry):
        rows = rows_at(i * 256, 256, 256)
        floats = src[rows, :].astype(F32)
        length = jnp.sqrt(jnp.sum(floats * floats, axis=1, keepdims=True) + epsilon)
        dst[rows, :] = (floats / length).astype(BF16)
        return carry

    lax.fori_loop(0, CROPS // 256, body, 0)


def normalise_columns(src, dst, dst_t):
    def body(i, carry):
        cols = rows_at(i * 256, 256, 256)
        floats = src[:, cols].astype(F32)
        length = jnp.sqrt(jnp.sum(floats * floats, axis=0, keepdims=True) + epsilon)
        unit = floats / length
        dst[:, cols] = unit.astype(BF16)
        dst_t[cols, :] = unit.T.astype(BF16)
        return carry

    lax.fori_loop(0, PROTOS // 256, body, 0)


def exp_tiles(rows_ref, cols_ref, out, rate, transposed):
    count, width = out.shape
    dims = (((1,), (1,)), ((), ())) if transposed else (((1,), (0,)), ((), ()))

    def body(i, total):
        rows = rows_at(i * 256, 256, 256)
        logits = lax.dot_general(rows_ref[rows, :], cols_ref[...], dims, preferred_element_type=F32)
        values = jnp.exp(logits * rate)
        out[rows, :] = values.astype(BF16)
        return total + jnp.sum(values.reshape(32, 8, width), axis=0)

    total = lax.fori_loop(0, count // 256, body, jnp.zeros((8, width), F32))
    return jnp.sum(total, axis=0, keepdims=True)


def vector_times(vector, matrix):
    high = vector.astype(BF16).astype(F32)
    low = vector - high
    row = lax.broadcasted_iota(jnp.int32, (16, vector.shape[1]), 0)
    left = jnp.where(row == 0, high, jnp.where(row == 1, low, 0.0)).astype(BF16)
    return jnp.sum(jnp.dot(left, matrix[...], preferred_element_type=F32), axis=0, keepdims=True)


def to_rows(vector, dst):
    for i in range(vector.shape[1] // 128):
        part = vector[:, i * 128 : (i + 1) * 128]
        dst[i * 128 : (i + 1) * 128, :] = jnp.broadcast_to(part, (128, 128)).T


def wide(narrow):
    return jnp.concatenate([narrow, narrow], axis=1)


def kernel(
    sf, tf, sp, tp, fg_out, pg_out,
    E, ET, S, ST, sh, th, ph, phT, ah, ahT,
    scaled_s, scaled_p, row_scale, col_scale, a_scale,
    F1, F2, P1,
    col_src, col_recv, row_part, row_sib, row_src, row_recv,
    own, snd_r, snd_l, rcv_r, rcv_l, pg,
    f_sib, f_recv, fg,
    col_s, col_r, rc_s, rc_r, rp_s, rp_r,
    rsr_s, rsr_r, rsl_s, rsl_r, agr_s, agr_r, agl_s, agl_r,
    fc_s, fc_r, fx_s, fx_r, fa_s, fa_r, ff_s, ff_r, po_s, fo_s,
):
    z = lax.axis_index("batch")
    p = lax.axis_index("proto")
    core = lax.rem(p, 2)
    chip = p // 2
    sibling = (z, chip * 2 + 1 - core)
    right = (lax.rem(z + 1, Z), p)
    left = (lax.rem(z + Z - 1, Z), p)

    def same_core(d):
        return (z, lax.rem(chip + d, CHIPS) * 2 + core)

    barrier = pltpu.get_barrier_semaphore()

    def greet_z(d, carry):
        pl.semaphore_signal(barrier, inc=1, device_id=(lax.rem(z + d, Z), p), device_id_type=MESH)
        return carry

    lax.fori_loop(1, Z, greet_z, 0)

    def greet_plane(d, carry):
        pl.semaphore_signal(barrier, inc=1, device_id=same_core(d), device_id_type=MESH)
        return carry

    lax.fori_loop(1, CHIPS, greet_plane, 0)
    pl.semaphore_signal(barrier, inc=1, device_id=sibling, device_id_type=MESH)

    def remote(src, dst, ss, rs, target):
        return pltpu.make_async_remote_copy(
            src_ref=src, dst_ref=dst, send_sem=ss, recv_sem=rs, device_id=target, device_id_type=MESH
        )

    def col_copy(i, d):
        return remote(
            col_src.at[i], col_recv.at[i, d - 1], col_s.at[i, d - 1], col_r.at[i, d - 1],
            (lax.rem(z + d, Z), p),
        )

    def col_send(i, partial):
        col_src[i] = partial
        for d in (4, 3, 5, 2, 6, 1, 7):
            col_copy(i, d).start()

    def col_total(i):
        for d in (1, 7, 2, 6, 3, 5, 4):
            col_copy(i, d).wait_recv()
        return col_src[i] + jnp.sum(col_recv[i], axis=0)

    def pair_copy(i):
        return remote(row_part.at[i], row_sib.at[i], rc_s.at[i], rc_r.at[i], sibling)

    def chip_copy(i, d):
        return remote(
            row_src.at[i], row_recv.at[i, d - 1], rp_s.at[i, d - 1], rp_r.at[i, d - 1], same_core(d)
        )

    def row_send(i, partial):
        row_part[i] = partial
        pair_copy(i).start()
        pair_copy(i).wait_recv()
        row_src[i] = row_part[i] + row_sib[i]
        for d in range(1, CHIPS):
            chip_copy(i, d).start()

    def row_total(i):
        for d in range(1, CHIPS):
            chip_copy(i, d).wait_recv()
        return row_src[i] + jnp.sum(row_recv[i], axis=0)

    normalise_rows(tf, th)
    normalise_columns(tp, ah, ahT)
    partial = exp_tiles(th, ah, E, teacher_rate, False)
    pl.semaphore_wait(barrier, Z - 1 + CHIPS - 1 + 1)

    col_send(0, partial)
    exp_tiles(ahT, th, ET, teacher_rate, True)
    scale = 1.0 / col_total(0)

    row_send(0, vector_times(scale, ET))
    normalise_rows(sf, sh)
    normalise_columns(sp, ph, phT)
    student_partial = exp_tiles(phT, sh, ST, student_rate, True)
    scale = 1.0 / row_total(0)

    col_send(1, vector_times(scale, E))
    row_send(3, student_partial)
    exp_tiles(sh, ph, S, student_rate, False)
    scale = 1.0 / col_total(1)

    row_send(1, vector_times(scale, ET))

    def student_features(i, carry):
        rows = rows_at(i * 256, 256, 256)
        F1[rows, :] = jnp.dot(S[rows, :], phT[...], preferred_element_type=F32)
        return carry

    lax.fori_loop(0, CROPS // 256, student_features, 0)
    scale = 1.0 / row_total(1)

    col_send(2, vector_times(scale, E))
    to_rows(grad_scale / row_total(3), a_scale)
    scaled_s[...] = (sh[...].astype(F32) * wide(a_scale[...])).astype(BF16)

    def student_protos(i, carry):
        rows = rows_at(i * 256, 256, 256)
        P1[rows, :] = jnp.dot(ST[rows, :], scaled_s[...], preferred_element_type=F32)
        return carry

    lax.fori_loop(0, PROTOS // 256, student_protos, 0)
    scale = 1.0 / col_total(2)

    row_send(2, vector_times(scale, ET))
    to_rows(scale, col_scale)
    scaled_p[...] = (phT[...].astype(F32) * wide(col_scale[...])).astype(BF16)

    def teacher_features(i, carry):
        rows = rows_at(i * 256, 256, 256)
        F2[rows, :] = jnp.dot(E[rows, :], scaled_p[...], preferred_element_type=F32)
        return carry

    lax.fori_loop(0, CROPS // 256, teacher_features, 0)
    to_rows(grad_scale / row_total(2), row_scale)
    scaled_s[...] = (sh[...].astype(F32) * wide(row_scale[...])).astype(BF16)

    def chunk(index):
        rows = rows_at(index * OWN, OWN, OWN)
        product = jnp.dot(ET[rows, :], scaled_s[...], preferred_element_type=F32)
        return P1[rows, :] - wide(col_scale[rows, :]) * product

    def ahead(d):
        return lax.rem(z + d, Z)

    def part(values, j):
        return values[j * SUB : (j + 1) * SUB, :]

    def rs_r(d, j):
        return remote(snd_r.at[d - 1, j], rcv_r.at[d - 1, j], rsr_s.at[d - 1, j], rsr_r.at[d - 1, j], right)

    def rs_l(d, j):
        return remote(snd_l.at[d - 1, j], rcv_l.at[d - 1, j], rsl_s.at[d - 1, j], rsl_r.at[d - 1, j], left)

    values = chunk(ahead(4))
    for j in (0, 1):
        snd_r[3, j] = part(values, j)
        rs_r(4, j).start()
    for j in (2, 3):
        snd_l[3, j] = part(values, j)
        rs_l(4, j).start()
    values = chunk(ahead(3))
    for j in (2, 3):
        snd_r[2, j] = part(values, j)
        rs_r(3, j).start()
    for j in (0, 1):
        snd_r[2, j] = part(values, j)
    values = chunk(ahead(Z - 3))
    for j in (0, 1):
        snd_l[2, j] = part(values, j)
        rs_l(3, j).start()
    for j in (2, 3):
        snd_l[2, j] = part(values, j)

    F1[...] = F1[...] * wide(a_scale[...]) - F2[...] * wide(row_scale[...])
    feature_pair = remote(F1.at[rows_at((1 - core) * HALF, HALF, HALF)], f_sib, fc_s, fc_r, sibling)
    feature_pair.start()

    for d in (2, 1):
        values = chunk(ahead(d))
        for j in range(4):
            snd_r[d - 1, j] = part(values, j)
        values = chunk(ahead(Z - d))
        for j in range(4):
            snd_l[d - 1, j] = part(values, j)
    values = chunk(z)
    for j in range(4):
        own[j] = part(values, j)

    def pass_on(d, j_right, j_left):
        for j in j_right:
            rs_r(d + 1, j).wait_recv()
            snd_r[d - 1, j] = snd_r[d - 1, j] + rcv_r[d, j]
            rs_r(d, j).start()
        for j in j_left:
            rs_l(d + 1, j).wait_recv()
            snd_l[d - 1, j] = snd_l[d - 1, j] + rcv_l[d, j]
            rs_l(d, j).start()

    pass_on(3, (0, 1), (2, 3))
    pass_on(2, (2, 3), (0, 1))

    feature_pair.wait_recv()
    mine = rows_at(core * HALF, HALF, HALF)
    F2[mine, :] = F1[mine, :] + f_sib[...]

    def piece(c):
        return rows_at(core * HALF + c * PIECE, PIECE, PIECE)

    def piece_copy(d):
        return remote(
            F2.at[piece(lax.rem(chip + d, CHIPS))], f_recv.at[d - 1], fx_s.at[d - 1], fx_r.at[d - 1],
            same_core(d),
        )

    for d in range(1, CHIPS):
        piece_copy(d).start()

    pass_on(2, (0, 1), (2, 3))
    pass_on(1, (2, 3), (0, 1))
    pass_on(1, (0, 1), (2, 3))

    def ag_r(d, j):
        block = pg.at[rows_at(lax.rem(z + Z - (d - 1), Z) * OWN + j * SUB, SUB, SUB)]
        return remote(block, block, agr_s.at[d - 1, j], agr_r.at[d - 1, j], right)

    def ag_l(d, j):
        block = pg.at[rows_at(lax.rem(z + (d - 1), Z) * OWN + j * SUB, SUB, SUB)]
        return remote(block, block, agl_s.at[d - 1, j], agl_r.at[d - 1, j], left)

    def finish(j):
        rows = rows_at(z * OWN + j * SUB, SUB, SUB)
        terms = own[j] + rcv_r[0, j] + rcv_l[0, j]
        floats = sp[:, rows_at(z * OWN, OWN, OWN)].astype(F32).T[j * SUB : (j + 1) * SUB, :]
        length = jnp.sqrt(jnp.sum(floats * floats, axis=1, keepdims=True) + epsilon)
        unit = floats / length
        pg[rows, :] = (terms - unit * jnp.sum(unit * terms, axis=1, keepdims=True)) / length
        ag_r(1, j).start()
        ag_l(1, j).start()

    for j in (2, 3):
        rs_r(1, j).wait_recv()
    for j in (0, 1):
        rs_l(1, j).wait_recv()
    for j in (0, 1):
        rs_r(1, j).wait_recv()
        finish(j)
    for j in (2, 3):
        rs_l(1, j).wait_recv()
        finish(j)

    def out_copy(owner):
        rows = rows_at(owner * OWN, OWN, OWN)
        return pltpu.make_async_copy(pg.at[rows], pg_out.at[rows], po_s.at[owner])

    for d in range(1, CHIPS):
        piece_copy(d).wait_recv()
    my_piece = piece(chip)
    terms = F2[my_piece, :] + jnp.sum(f_recv[...], axis=0)
    floats = sf[my_piece, :].astype(F32)
    length = jnp.sqrt(jnp.sum(floats * floats, axis=1, keepdims=True) + epsilon)
    unit = floats / length
    fg[my_piece, :] = (terms - unit * jnp.sum(unit * terms, axis=1, keepdims=True)) / length

    def spread_copy(d):
        return remote(fg.at[my_piece], fg.at[my_piece], fa_s.at[d - 1], fa_r.at[d - 1], same_core(d))

    def arrived_copy(d):
        block = fg.at[piece(lax.rem(chip + CHIPS - d, CHIPS))]
        return remote(block, block, fa_s.at[d - 1], fa_r.at[d - 1], same_core(d))

    def hand_copy(d):
        block = fg.at[piece(lax.rem(chip + CHIPS - d, CHIPS))]
        return remote(block, block, ff_s.at[d], ff_r.at[d], sibling)

    def hand_arrived(d):
        start = (1 - core) * HALF + lax.rem(chip + CHIPS - d, CHIPS) * PIECE
        block = fg.at[rows_at(start, PIECE, PIECE)]
        return remote(block, block, ff_s.at[d], ff_r.at[d], sibling)

    for d in range(1, CHIPS):
        spread_copy(d).start()
    hand_copy(0).start()

    def arrived_r(d, j):
        block = pg.at[rows_at(lax.rem(z + Z - d, Z) * OWN + j * SUB, SUB, SUB)]
        return remote(block, block, agr_s.at[d - 1, j], agr_r.at[d - 1, j], right)

    def arrived_l(d, j):
        block = pg.at[rows_at(lax.rem(z + d, Z) * OWN + j * SUB, SUB, SUB)]
        return remote(block, block, agl_s.at[d - 1, j], agl_r.at[d - 1, j], left)

    out_copy(z).start()
    for d in (1, 2):
        for j in range(4):
            arrived_r(d, j).wait_recv()
            ag_r(d + 1, j).start()
            arrived_l(d, j).wait_recv()
            ag_l(d + 1, j).start()
        out_copy(lax.rem(z + Z - d, Z)).start()
        out_copy(lax.rem(z + d, Z)).start()
    for j in (0, 1):
        arrived_r(3, j).wait_recv()
        ag_r(4, j).start()
        arrived_l(3, j).wait_recv()
    for j in (2, 3):
        arrived_l(3, j).wait_recv()
        ag_l(4, j).start()
        arrived_r(3, j).wait_recv()
    out_copy(lax.rem(z + Z - 3, Z)).start()
    out_copy(lax.rem(z + 3, Z)).start()

    for d in range(1, CHIPS):
        arrived_copy(d).wait_recv()
        hand_copy(d).start()

    for j in (0, 1):
        arrived_r(4, j).wait_recv()
    for j in (2, 3):
        arrived_l(4, j).wait_recv()
    out_copy(lax.rem(z + 4, Z)).start()

    for d in range(CHIPS):
        hand_arrived(d).wait_recv()
    feature_out = pltpu.make_async_copy(fg, fg_out, fo_s)
    feature_out.start()

    for i in range(3):
        for d in range(1, Z):
            col_copy(i, d).wait_send()
    for i in range(4):
        pair_copy(i).wait_send()
        for d in range(1, CHIPS):
            chip_copy(i, d).wait_send()
    for d in (4, 3, 2, 1):
        for j in range(4):
            if d < 4 or j in (0, 1):
                rs_r(d, j).wait_send()
                ag_r(d, j).wait_send()
            if d < 4 or j in (2, 3):
                rs_l(d, j).wait_send()
                ag_l(d, j).wait_send()
    feature_pair.wait_send()
    for d in range(1, CHIPS):
        piece_copy(d).wait_send()
        spread_copy(d).wait_send()
    for d in range(CHIPS):
        hand_copy(d).wait_send()
    for owner in range(Z):
        out_copy(owner).wait()
    feature_out.wait()


def on_device(student_features, teacher_features, student_protos, teacher_protos):
    vmem = pltpu.VMEM
    dma = pltpu.SemaphoreType.DMA
    return pl.pallas_call(
        kernel,
        out_shape=(
            jax.ShapeDtypeStruct((CROPS, D), F32),
            jax.ShapeDtypeStruct((PROTOS, D), F32),
        ),
        in_specs=[pl.BlockSpec(memory_space=pltpu.VMEM)] * 4,
        out_specs=[pl.BlockSpec(memory_space=pl.ANY)] * 2,
        scratch_shapes=[
            vmem((CROPS, PROTOS), BF16),
            vmem((PROTOS, CROPS), BF16),
            vmem((CROPS, PROTOS), BF16),
            vmem((PROTOS, CROPS), BF16),
            vmem((CROPS, D), BF16),
            vmem((CROPS, D), BF16),
            vmem((D, PROTOS), BF16),
            vmem((PROTOS, D), BF16),
            vmem((D, PROTOS), BF16),
            vmem((PROTOS, D), BF16),
            vmem((CROPS, D), BF16),
            vmem((PROTOS, D), BF16),
            vmem((CROPS, 128), F32),
            vmem((PROTOS, 128), F32),
            vmem((CROPS, 128), F32),
            vmem((CROPS, D), F32),
            vmem((CROPS, D), F32),
            vmem((PROTOS, D), F32),
            vmem((3, 1, PROTOS), F32),
            vmem((3, Z - 1, 1, PROTOS), F32),
            vmem((4, 1, CROPS), F32),
            vmem((4, 1, CROPS), F32),
            vmem((4, 1, CROPS), F32),
            vmem((4, CHIPS - 1, 1, CROPS), F32),
            vmem((4, SUB, D), F32),
            vmem((4, 4, SUB, D), F32),
            vmem((4, 4, SUB, D), F32),
            vmem((4, 4, SUB, D), F32),
            vmem((4, 4, SUB, D), F32),
            vmem((PROTOS, D), F32),
            vmem((HALF, D), F32),
            vmem((CHIPS - 1, PIECE, D), F32),
            vmem((CROPS, D), F32),
            dma((3, Z - 1)),
            dma((3, Z - 1)),
            dma((4,)),
            dma((4,)),
            dma((4, CHIPS - 1)),
            dma((4, CHIPS - 1)),
        ]
        + [dma((4, 4))] * 8
        + [
            dma,
            dma,
            dma((CHIPS - 1,)),
            dma((CHIPS - 1,)),
            dma((CHIPS - 1,)),
            dma((CHIPS - 1,)),
            dma((CHIPS,)),
            dma((CHIPS,)),
            dma((Z,)),
            dma,
        ],
        compiler_params=pltpu.CompilerParams(
            collective_id=0, has_side_effects=True, vmem_limit_bytes=60 * 2**20
        ),
    )(student_features, teacher_features, student_protos, teacher_protos)


def solution(mesh):
    return jax.shard_map(
        on_device,
        mesh=mesh,
        in_specs=(P("batch", None), P("batch", None), P(None, "proto"), P(None, "proto")),
        out_specs=(P("batch", None), P("proto", None)),
        check_vma=False,
    )
```

time: 586 us -> 102 us (0.17)
  blocking collectives: 299 us -> 0 us
  waiting for transfers between devices: 185 us -> 0 us
  Pallas kernels: 0 us -> 97.6 us
  other arithmetic: 57.4 us -> 0 us
  matrix products: 23.4 us -> 0 us
  between operations: 14.2 us -> 0.65 us
    psum x6 -> x0, blocking collectives: 299 us -> none  [the longest x3 258 us: on_device(): row_total = lax.psum(partial_rows, 'proto')]
    psum x2 -> x0, waiting for transfers between devices: 185 us -> none  [the longest x1 108 us: on_device(): lax.psum(jnp.dot(grad_logits, proto_half, preferred_element_type=jnp.floa...]
    pallas_call x0 -> x1, Pallas kernels: none -> 97.6 us  [on_device(): pl.pallas_call(kernel, out_shape=(jax.ShapeDtypeStruct((CROPS, D), F32),...]
    reduce_sum x11 -> x0, other arithmetic: 39.7 us -> none  [the longest x3 18.5 us: on_device(): partial_rows = jnp.sum(weights, axis=1)]
    dot_general x4 -> x0, matrix products: 23.4 us -> none  [the longest x1 8.24 us: on_device(): lax.dot_general(teacher_half, anchor_half, contract_last, preferred_eleme...]
    convert_element_type x1 -> x0, other arithmetic: 11.5 us -> none  [on_device(): (loss_scale * (predicted - weights) / student_temp).astype(jnp.bfloat16)]
    div x2 -> x0, other arithmetic: 6.2 us -> none  [project_back(): (grads - unit * jnp.sum(unit * grads, axis=1, keepdims=True)) / length]
  transfers between devices with their start and end apart: 2 -> 0, of which waited for: 2 -> 0; matrix products, arithmetic and copies ran while one was open for 2% -> 0% of each run, Pallas kernels for 0% -> 0%
where the time goes in v1:
time: 102 us
  Pallas kernels  97.6 us (96%)
  local copies, waits for them, and re-layouts  4.12 us (4%)
    pallas_call x1, Pallas kernels, on_device(): pl.pallas_call(kernel, out_shape=(jax.ShapeDtypeStruct((CROPS, D), F32),...  97.6 us
    unnamed x4, local copies, waits for them, and re-layouts  4.12 us

profile of v1, /device:TPU:1, one launch (start us, length us, event | category | flops | bytes accessed | tf_op | source)
XLA Modules:
  0.0 102.3 jit_solution(11734845542857272903)
XLA Ops:
  0.6 97.6 %shard_map.59 = (f32[1536,256]{1,0:T(8,128)}, f32[2048,256]{1,0:T(8,128)}) custom-call(bf16[1536,256]{1,0:T(8,128)(2,1)} %sf.1, bf16[1536,256]{1,0:T(8,128)(2,1)} %tf.1, bf16[256,2048]{1,0:T(8,128)(2,1)} %sp.1, bf16[256,2048]{1,0:T(8,128)(2,1)} %tp.1), custom_call_target="tpu_custom_call" | custom-call | tf_op jit(solution)/shard_map/pallas_call | solution.py:443
  98.2 0.0 copy-start
  98.2 2.8 %copy.8 = f32[1536,256]{1,0:T(8,128)} copy(f32[1536,256]{1,0:T(8,128)} %get-tuple-element.4) | data formatting | bytes 3145728
  101.0 0.0 copy-done
  101.0 1.3 %copy.9 = f32[2048,256]{1,0:T(8,128)} copy(f32[2048,256]{1,0:T(8,128)S(1)} %copy-done) | data formatting | bytes 4194304
Async XLA Ops:
  98.2 2.8 %copy-start = (f32[2048,256]{1,0:T(8,128)S(1)}, f32[2048,256]{1,0:T(8,128)}, u32[]{:S(2)}) copy-start(f32[2048,256]{1,0:T(8,128)} %get-tuple-element.5) | copy-start | bytes 6291460

commit v2 on v1

--- a/solution.py
+++ b/solution.py
@@ -10,8 +10,9 @@
 BF16 = jnp.bfloat16
 
 epsilon = 1e-06
-teacher_rate = 25.0
-student_rate = 10.0
+log2_e = 1.4426950408889634
+teacher_rate = 25.0 * log2_e
+student_rate = 10.0 * log2_e
 grad_scale = 40960.0
 
 CROPS = 1536
@@ -40,14 +41,21 @@
     lax.fori_loop(0, CROPS // 256, body, 0)
 
 
-def normalise_columns(src, dst, dst_t):
+def normalise_columns(src, dst):
     def body(i, carry):
         cols = rows_at(i * 256, 256, 256)
         floats = src[:, cols].astype(F32)
         length = jnp.sqrt(jnp.sum(floats * floats, axis=0, keepdims=True) + epsilon)
-        unit = floats / length
-        dst[:, cols] = unit.astype(BF16)
-        dst_t[cols, :] = unit.T.astype(BF16)
+        dst[:, cols] = (floats / length).astype(BF16)
+        return carry
+
+    lax.fori_loop(0, PROTOS // 256, body, 0)
+
+
+def transpose_into(src, dst):
+    def body(i, carry):
+        cols = rows_at(i * 256, 256, 256)
+        dst[cols, :] = src[:, cols].astype(F32).T.astype(BF16)
         return carry
 
     lax.fori_loop(0, PROTOS // 256, body, 0)
@@ -55,16 +63,17 @@
 
 def exp_tiles(rows_ref, cols_ref, out, rate, transposed):
     count, width = out.shape
+    block = count // 2
     dims = (((1,), (1,)), ((), ())) if transposed else (((1,), (0,)), ((), ()))
 
     def body(i, total):
-        rows = rows_at(i * 256, 256, 256)
+        rows = rows_at(i * block, block, block)
         logits = lax.dot_general(rows_ref[rows, :], cols_ref[...], dims, preferred_element_type=F32)
-        values = jnp.exp(logits * rate)
+        values = jnp.exp2(logits * rate)
         out[rows, :] = values.astype(BF16)
-        return total + jnp.sum(values.reshape(32, 8, width), axis=0)
-
-    total = lax.fori_loop(0, count // 256, body, jnp.zeros((8, width), F32))
+        return total + jnp.sum(values.reshape(block // 8, 8, width), axis=0)
+
+    total = lax.fori_loop(0, 2, body, jnp.zeros((8, width), F32))
     return jnp.sum(total, axis=0, keepdims=True)
 
 
@@ -86,17 +95,32 @@
     return jnp.concatenate([narrow, narrow], axis=1)
 
 
+def scale_rows(values, scale, dst):
+    dst[...] = (values[...].astype(F32) * wide(scale[...])).astype(BF16)
+
+
+def products(matrix, columns, dst):
+    block = dst.shape[0] // 2
+
+    def body(i, carry):
+        rows = rows_at(i * block, block, block)
+        dst[rows, :] = jnp.dot(matrix[rows, :], columns[...], preferred_element_type=F32)
+        return carry
+
+    lax.fori_loop(0, 2, body, 0)
+
+
 def kernel(
-    sf, tf, sp, tp, fg_out, pg_out,
+    sf_in, tf_in, sp_in, tp_in, fg, pg, sf, tf, sp, tp,
     E, ET, S, ST, sh, th, ph, phT, ah, ahT,
     scaled_s, scaled_p, row_scale, col_scale, a_scale,
     F1, F2, P1,
     col_src, col_recv, row_part, row_sib, row_src, row_recv,
-    own, snd_r, snd_l, rcv_r, rcv_l, pg,
-    f_sib, f_recv, fg,
+    own, snd_r, snd_l, rcv_r, rcv_l, own_unit, own_len,
+    f_sib, f_recv, in_s,
     col_s, col_r, rc_s, rc_r, rp_s, rp_r,
     rsr_s, rsr_r, rsl_s, rsl_r, agr_s, agr_r, agl_s, agl_r,
-    fc_s, fc_r, fx_s, fx_r, fa_s, fa_r, ff_s, ff_r, po_s, fo_s,
+    fc_s, fc_r, fx_s, fx_r, fa_s, fa_r, ff_s, ff_r,
 ):
     z = lax.axis_index("batch")
     p = lax.axis_index("proto")
@@ -124,6 +148,14 @@
     lax.fori_loop(1, CHIPS, greet_plane, 0)
     pl.semaphore_signal(barrier, inc=1, device_id=sibling, device_id_type=MESH)
 
+    def load(i):
+        src = (tf_in, tp_in, sf_in, sp_in)[i]
+        dst = (tf, tp, sf, sp)[i]
+        return pltpu.make_async_copy(src, dst, in_s.at[i])
+
+    for i in range(4):
+        load(i).start()
+
     def remote(src, dst, ss, rs, target):
         return pltpu.make_async_remote_copy(
             src_ref=src, dst_ref=dst, send_sem=ss, recv_sem=rs, device_id=target, device_id_type=MESH
@@ -166,60 +198,52 @@
             chip_copy(i, d).wait_recv()
         return row_src[i] + jnp.sum(row_recv[i], axis=0)
 
+    load(0).wait()
     normalise_rows(tf, th)
-    normalise_columns(tp, ah, ahT)
+    load(1).wait()
+    normalise_columns(tp, ah)
     partial = exp_tiles(th, ah, E, teacher_rate, False)
     pl.semaphore_wait(barrier, Z - 1 + CHIPS - 1 + 1)
 
     col_send(0, partial)
+    transpose_into(ah, ahT)
     exp_tiles(ahT, th, ET, teacher_rate, True)
     scale = 1.0 / col_total(0)
 
     row_send(0, vector_times(scale, ET))
+    load(2).wait()
     normalise_rows(sf, sh)
-    normalise_columns(sp, ph, phT)
+    load(3).wait()
+    normalise_columns(sp, ph)
+    transpose_into(ph, phT)
+    floats = sp[:, rows_at(z * OWN, OWN, OWN)].astype(F32).T
+    length = jnp.sqrt(jnp.sum(floats * floats, axis=1, keepdims=True) + epsilon)
+    own_len[...] = jnp.broadcast_to(length, (OWN, 128))
+    own_unit[...] = floats / length
+    scale = 1.0 / row_total(0)
+
+    col_send(1, vector_times(scale, E))
     student_partial = exp_tiles(phT, sh, ST, student_rate, True)
-    scale = 1.0 / row_total(0)
-
-    col_send(1, vector_times(scale, E))
-    row_send(3, student_partial)
     exp_tiles(sh, ph, S, student_rate, False)
     scale = 1.0 / col_total(1)
 
     row_send(1, vector_times(scale, ET))
-
-    def student_features(i, carry):
-        rows = rows_at(i * 256, 256, 256)
-        F1[rows, :] = jnp.dot(S[rows, :], phT[...], preferred_element_type=F32)
-        return carry
-
-    lax.fori_loop(0, CROPS // 256, student_features, 0)
+    row_send(3, student_partial)
+    products(S, phT, F1)
     scale = 1.0 / row_total(1)
 
     col_send(2, vector_times(scale, E))
     to_rows(grad_scale / row_total(3), a_scale)
-    scaled_s[...] = (sh[...].astype(F32) * wide(a_scale[...])).astype(BF16)
-
-    def student_protos(i, carry):
-        rows = rows_at(i * 256, 256, 256)
-        P1[rows, :] = jnp.dot(ST[rows, :], scaled_s[...], preferred_element_type=F32)
-        return carry
-
-    lax.fori_loop(0, PROTOS // 256, student_protos, 0)
+    scale_rows(sh, a_scale, scaled_s)
+    products(ST, scaled_s, P1)
     scale = 1.0 / col_total(2)
 
     row_send(2, vector_times(scale, ET))
     to_rows(scale, col_scale)
-    scaled_p[...] = (phT[...].astype(F32) * wide(col_scale[...])).astype(BF16)
-
-    def teacher_features(i, carry):
-        rows = rows_at(i * 256, 256, 256)
-        F2[rows, :] = jnp.dot(E[rows, :], scaled_p[...], preferred_element_type=F32)
-        return carry
-
-    lax.fori_loop(0, CROPS // 256, teacher_features, 0)
+    scale_rows(phT, col_scale, scaled_p)
+    products(E, scaled_p, F2)
     to_rows(grad_scale / row_total(2), row_scale)
-    scaled_s[...] = (sh[...].astype(F32) * wide(row_scale[...])).astype(BF16)
+    scale_rows(sh, row_scale, scaled_s)
 
     def chunk(index):
         rows = rows_at(index * OWN, OWN, OWN)
@@ -261,17 +285,6 @@
     F1[...] = F1[...] * wide(a_scale[...]) - F2[...] * wide(row_scale[...])
     feature_pair = remote(F1.at[rows_at((1 - core) * HALF, HALF, HALF)], f_sib, fc_s, fc_r, sibling)
     feature_pair.start()
-
-    for d in (2, 1):
-        values = chunk(ahead(d))
-        for j in range(4):
-            snd_r[d - 1, j] = part(values, j)
-        values = chunk(ahead(Z - d))
-        for j in range(4):
-            snd_l[d - 1, j] = part(values, j)
-    values = chunk(z)
-    for j in range(4):
-        own[j] = part(values, j)
 
     def pass_on(d, j_right, j_left):
         for j in j_right:
@@ -283,8 +296,20 @@
             snd_l[d - 1, j] = snd_l[d - 1, j] + rcv_l[d, j]
             rs_l(d, j).start()
 
+    def own_terms(d):
+        values = chunk(ahead(d))
+        for j in range(4):
+            snd_r[d - 1, j] = part(values, j)
+        values = chunk(ahead(Z - d))
+        for j in range(4):
+            snd_l[d - 1, j] = part(values, j)
+
+    own_terms(2)
     pass_on(3, (0, 1), (2, 3))
-    pass_on(2, (2, 3), (0, 1))
+    own_terms(1)
+    values = chunk(z)
+    for j in range(4):
+        own[j] = part(values, j)
 
     feature_pair.wait_recv()
     mine = rows_at(core * HALF, HALF, HALF)
@@ -299,12 +324,23 @@
             same_core(d),
         )
 
-    for d in range(1, CHIPS):
+    for d in range(1, 5):
         piece_copy(d).start()
-
+    pass_on(2, (2, 3), (0, 1))
+    for d in range(5, 12):
+        piece_copy(d).start()
     pass_on(2, (0, 1), (2, 3))
+    for d in range(12, CHIPS):
+        piece_copy(d).start()
     pass_on(1, (2, 3), (0, 1))
+    for i in range(3):
+        for d in range(1, Z):
+            col_copy(i, d).wait_send()
     pass_on(1, (0, 1), (2, 3))
+    for i in range(4):
+        pair_copy(i).wait_send()
+        for d in range(1, CHIPS):
+            chip_copy(i, d).wait_send()
 
     def ag_r(d, j):
         block = pg.at[rows_at(lax.rem(z + Z - (d - 1), Z) * OWN + j * SUB, SUB, SUB)]
@@ -317,9 +353,8 @@
     def finish(j):
         rows = rows_at(z * OWN + j * SUB, SUB, SUB)
         terms = own[j] + rcv_r[0, j] + rcv_l[0, j]
-        floats = sp[:, rows_at(z * OWN, OWN, OWN)].astype(F32).T[j * SUB : (j + 1) * SUB, :]
-        length = jnp.sqrt(jnp.sum(floats * floats, axis=1, keepdims=True) + epsilon)
-        unit = floats / length
+        length = wide(own_len[j * SUB : (j + 1) * SUB, :])
+        unit = own_unit[j * SUB : (j + 1) * SUB, :]
         pg[rows, :] = (terms - unit * jnp.sum(unit * terms, axis=1, keepdims=True)) / length
         ag_r(1, j).start()
         ag_l(1, j).start()
@@ -334,10 +369,6 @@
     for j in (2, 3):
         rs_l(1, j).wait_recv()
         finish(j)
-
-    def out_copy(owner):
-        rows = rows_at(owner * OWN, OWN, OWN)
-        return pltpu.make_async_copy(pg.at[rows], pg_out.at[rows], po_s.at[owner])
 
     for d in range(1, CHIPS):
         piece_copy(d).wait_recv()
@@ -376,15 +407,22 @@
         block = pg.at[rows_at(lax.rem(z + d, Z) * OWN + j * SUB, SUB, SUB)]
         return remote(block, block, agl_s.at[d - 1, j], agl_r.at[d - 1, j], left)
 
-    out_copy(z).start()
+    feature_pair.wait_send()
     for d in (1, 2):
         for j in range(4):
             arrived_r(d, j).wait_recv()
             ag_r(d + 1, j).start()
             arrived_l(d, j).wait_recv()
             ag_l(d + 1, j).start()
-        out_copy(lax.rem(z + Z - d, Z)).start()
-        out_copy(lax.rem(z + d, Z)).start()
+        for i in (4, 3) if d == 1 else (2, 1):
+            for j in range(4):
+                if i < 4 or j in (0, 1):
+                    rs_r(i, j).wait_send()
+                if i < 4 or j in (2, 3):
+                    rs_l(i, j).wait_send()
+        if d == 1:
+            for i in range(1, CHIPS):
+                piece_copy(i).wait_send()
     for j in (0, 1):
         arrived_r(3, j).wait_recv()
         ag_r(4, j).start()
@@ -393,62 +431,53 @@
         arrived_l(3, j).wait_recv()
         ag_l(4, j).start()
         arrived_r(3, j).wait_recv()
-    out_copy(lax.rem(z + Z - 3, Z)).start()
-    out_copy(lax.rem(z + 3, Z)).start()
 
     for d in range(1, CHIPS):
         arrived_copy(d).wait_recv()
         hand_copy(d).start()
+    for d in range(1, CHIPS):
+        spread_copy(d).wait_send()
 
     for j in (0, 1):
         arrived_r(4, j).wait_recv()
     for j in (2, 3):
         arrived_l(4, j).wait_recv()
-    out_copy(lax.rem(z + 4, Z)).start()
 
     for d in range(CHIPS):
         hand_arrived(d).wait_recv()
-    feature_out = pltpu.make_async_copy(fg, fg_out, fo_s)
-    feature_out.start()
-
-    for i in range(3):
-        for d in range(1, Z):
-            col_copy(i, d).wait_send()
-    for i in range(4):
-        pair_copy(i).wait_send()
-        for d in range(1, CHIPS):
-            chip_copy(i, d).wait_send()
+
     for d in (4, 3, 2, 1):
         for j in range(4):
             if d < 4 or j in (0, 1):
-                rs_r(d, j).wait_send()
                 ag_r(d, j).wait_send()
             if d < 4 or j in (2, 3):
-                rs_l(d, j).wait_send()
                 ag_l(d, j).wait_send()
-    feature_pair.wait_send()
-    for d in range(1, CHIPS):
-        piece_copy(d).wait_send()
-        spread_copy(d).wait_send()
     for d in range(CHIPS):
         hand_copy(d).wait_send()
-    for owner in range(Z):
-        out_copy(owner).wait()
-    feature_out.wait()
+
+
+def write_out(features, protos, features_out, protos_out, sems):
+    first = pltpu.make_async_copy(features, features_out, sems.at[0])
+    second = pltpu.make_async_copy(protos, protos_out, sems.at[1])
+    first.start()
+    second.start()
+    first.wait()
+    second.wait()
 
 
 def on_device(student_features, teacher_features, student_protos, teacher_protos):
     vmem = pltpu.VMEM
     dma = pltpu.SemaphoreType.DMA
-    return pl.pallas_call(
+    features, protos = pl.pallas_call(
         kernel,
-        out_shape=(
-            jax.ShapeDtypeStruct((CROPS, D), F32),
-            jax.ShapeDtypeStruct((PROTOS, D), F32),
-        ),
-        in_specs=[pl.BlockSpec(memory_space=pltpu.VMEM)] * 4,
-        out_specs=[pl.BlockSpec(memory_space=pl.ANY)] * 2,
+        out_shape=(pltpu.VMEM((CROPS, D), F32), pltpu.VMEM((PROTOS, D), F32)),
+        in_specs=[pl.BlockSpec(memory_space=pl.ANY)] * 4,
+        out_specs=[pl.BlockSpec(memory_space=pltpu.VMEM)] * 2,
         scratch_shapes=[
+            vmem((CROPS, D), BF16),
+            vmem((CROPS, D), BF16),
+            vmem((D, PROTOS), BF16),
+            vmem((D, PROTOS), BF16),
             vmem((CROPS, PROTOS), BF16),
             vmem((PROTOS, CROPS), BF16),
             vmem((CROPS, PROTOS), BF16),
@@ -478,10 +507,11 @@
             vmem((4, 4, SUB, D), F32),
             vmem((4, 4, SUB, D), F32),
             vmem((4, 4, SUB, D), F32),
-            vmem((PROTOS, D), F32),
+            vmem((OWN, D), F32),
+            vmem((OWN, 128), F32),
             vmem((HALF, D), F32),
             vmem((CHIPS - 1, PIECE, D), F32),
-            vmem((CROPS, D), F32),
+            dma((4,)),
             dma((3, Z - 1)),
             dma((3, Z - 1)),
             dma((4,)),
@@ -499,13 +529,25 @@
             dma((CHIPS - 1,)),
             dma((CHIPS,)),
             dma((CHIPS,)),
-            dma((Z,)),
-            dma,
         ],
         compiler_params=pltpu.CompilerParams(
-            collective_id=0, has_side_effects=True, vmem_limit_bytes=60 * 2**20
+            collective_id=0, has_side_effects=True, vmem_limit_bytes=52 * 2**20
         ),
     )(student_features, teacher_features, student_protos, teacher_protos)
+    return pl.pallas_call(
+        write_out,
+        out_shape=(
+            jax.ShapeDtypeStruct((CROPS, D), F32),
+            jax.ShapeDtypeStruct((PROTOS, D), F32),
+        ),
+        in_specs=[pl.BlockSpec(memory_space=pltpu.VMEM)] * 2,
+        out_specs=[pl.BlockSpec(memory_space=pl.ANY)] * 2,
+        scratch_shapes=[dma((2,))],
+        compiler_params=pltpu.CompilerParams(vmem_limit_bytes=2 * 2**20),
+    )(
+        pltpu.with_memory_space_constraint(features, pltpu.VMEM),
+        pltpu.with_memory_space_constraint(protos, pltpu.VMEM),
+    )
 
 
 def solution(mesh):

time: 102 us -> 96.4 us (0.945)
  local copies, waits for them, and re-layouts: 4.12 us -> 0 us
  Pallas kernels: 97.6 us -> 95.6 us
    unnamed x4 -> x0, local copies, waits for them, and re-layouts: 4.12 us -> none
    pallas_call x1 -> x2, Pallas kernels: 97.6 us -> 95.6 us  [the longest x1 93.7 us: on_device(): pl.pallas_call(kernel, out_shape=(pltpu.VMEM((CROPS, D), F32), pltpu.VMEM...]
where the time goes in v2:
time: 96.4 us
  Pallas kernels  95.6 us (99%)
    pallas_call x1, Pallas kernels, on_device(): pl.pallas_call(kernel, out_shape=(pltpu.VMEM((CROPS, D), F32), pltpu.VMEM...  93.7 us

profile of v2, /device:TPU:1, one launch (start us, length us, event | category | flops | bytes accessed | tf_op | source)
XLA Modules:
  0.0 96.4 jit_solution(3472779038095481214)
XLA Ops:
  0.6 93.7 %shard_map.59 = (f32[1536,256]{1,0:T(8,128)S(1)}, f32[2048,256]{1,0:T(8,128)S(1)}) custom-call(bf16[1536,256]{1,0:T(8,128)(2,1)} %sf_in.1, bf16[1536,256]{1,0:T(8,128)(2,1)} %tf_in.1, bf16[256,2048]{1,0:T(8,128)(2,1)} %sp_in.1, bf16[256,2048]{1,0:T(8,128)(2,1)} %tp_in.1), custom_call_target="tpu_custom_call" | custom-call | tf_op jit(solution)/shard_map/pallas_call | solution.py:471
  94.3 1.9 %shard_map.60 = (f32[1536,256]{1,0:T(8,128)}, f32[2048,256]{1,0:T(8,128)}) custom-call(f32[1536,256]{1,0:T(8,128)S(1)} %get-tuple-element.4.features, f32[2048,256]{1,0:T(8,128)S(1)} %get-tuple-element.5.protos), custom_call_target="tpu_custom_call" | custom-call | tf_op jit(solution)/shard_map/pallas_call | solution.py:537

commit v3 on v2

--- a/solution.py
+++ b/solution.py
@@ -21,9 +21,22 @@
 Z = 8
 CHIPS = 16
 OWN = PROTOS // Z
-SUB = OWN // 4
+SUBS = 4
+SUB = OWN // SUBS
+FIRST = tuple(range(SUBS // 2))
+LAST = tuple(range(SUBS // 2, SUBS))
 HALF = CROPS // 2
 PIECE = HALF // CHIPS
+
+
+def hops(offset):
+    return min(offset[0], 4 - offset[0]) + min(offset[1], 4 - offset[1])
+
+
+PLANE = sorted(
+    [(y, x) for y in range(4) for x in range(4) if y + x > 0],
+    key=lambda offset: (-hops(offset), offset),
+)
 
 
 def rows_at(start, size, step):
@@ -130,23 +143,18 @@
     right = (lax.rem(z + 1, Z), p)
     left = (lax.rem(z + Z - 1, Z), p)
 
+    def chip_at(d):
+        y = lax.rem(chip // 4 + PLANE[d - 1][0], 4)
+        x = lax.rem(chip + PLANE[d - 1][1], 4)
+        return y * 4 + x
+
+    def chip_from(d):
+        y = lax.rem(chip // 4 + 4 - PLANE[d - 1][0], 4)
+        x = lax.rem(chip + 4 - PLANE[d - 1][1], 4)
+        return y * 4 + x
+
     def same_core(d):
-        return (z, lax.rem(chip + d, CHIPS) * 2 + core)
-
-    barrier = pltpu.get_barrier_semaphore()
-
-    def greet_z(d, carry):
-        pl.semaphore_signal(barrier, inc=1, device_id=(lax.rem(z + d, Z), p), device_id_type=MESH)
-        return carry
-
-    lax.fori_loop(1, Z, greet_z, 0)
-
-    def greet_plane(d, carry):
-        pl.semaphore_signal(barrier, inc=1, device_id=same_core(d), device_id_type=MESH)
-        return carry
-
-    lax.fori_loop(1, CHIPS, greet_plane, 0)
-    pl.semaphore_signal(barrier, inc=1, device_id=sibling, device_id_type=MESH)
+        return (z, chip_at(d) * 2 + core)
 
     def load(i):
         src = (tf_in, tp_in, sf_in, sp_in)[i]
@@ -155,6 +163,22 @@
 
     for i in range(4):
         load(i).start()
+
+    barrier = pltpu.get_barrier_semaphore()
+
+    def greet_z(d, carry):
+        pl.semaphore_signal(barrier, inc=1, device_id=(lax.rem(z + d, Z), p), device_id_type=MESH)
+        return carry
+
+    lax.fori_loop(1, Z, greet_z, 0)
+
+    def greet_plane(d, carry):
+        target = (z, lax.rem(chip + d, CHIPS) * 2 + core)
+        pl.semaphore_signal(barrier, inc=1, device_id=target, device_id_type=MESH)
+        return carry
+
+    lax.fori_loop(1, CHIPS, greet_plane, 0)
+    pl.semaphore_signal(barrier, inc=1, device_id=sibling, device_id_type=MESH)
 
     def remote(src, dst, ss, rs, target):
         return pltpu.make_async_remote_copy(
@@ -194,7 +218,7 @@
             chip_copy(i, d).start()
 
     def row_total(i):
-        for d in range(1, CHIPS):
+        for d in reversed(range(1, CHIPS)):
             chip_copy(i, d).wait_recv()
         return row_src[i] + jnp.sum(row_recv[i], axis=0)
 
@@ -263,23 +287,23 @@
         return remote(snd_l.at[d - 1, j], rcv_l.at[d - 1, j], rsl_s.at[d - 1, j], rsl_r.at[d - 1, j], left)
 
     values = chunk(ahead(4))
-    for j in (0, 1):
+    for j in FIRST:
         snd_r[3, j] = part(values, j)
         rs_r(4, j).start()
-    for j in (2, 3):
+    for j in LAST:
         snd_l[3, j] = part(values, j)
         rs_l(4, j).start()
     values = chunk(ahead(3))
-    for j in (2, 3):
+    for j in LAST:
         snd_r[2, j] = part(values, j)
         rs_r(3, j).start()
-    for j in (0, 1):
+    for j in FIRST:
         snd_r[2, j] = part(values, j)
     values = chunk(ahead(Z - 3))
-    for j in (0, 1):
+    for j in FIRST:
         snd_l[2, j] = part(values, j)
         rs_l(3, j).start()
-    for j in (2, 3):
+    for j in LAST:
         snd_l[2, j] = part(values, j)
 
     F1[...] = F1[...] * wide(a_scale[...]) - F2[...] * wide(row_scale[...])
@@ -287,28 +311,27 @@
     feature_pair.start()
 
     def pass_on(d, j_right, j_left):
-        for j in j_right:
-            rs_r(d + 1, j).wait_recv()
-            snd_r[d - 1, j] = snd_r[d - 1, j] + rcv_r[d, j]
-            rs_r(d, j).start()
-        for j in j_left:
+        for i, j in zip(j_right, j_left):
+            rs_r(d + 1, i).wait_recv()
+            snd_r[d - 1, i] = snd_r[d - 1, i] + rcv_r[d, i]
+            rs_r(d, i).start()
             rs_l(d + 1, j).wait_recv()
             snd_l[d - 1, j] = snd_l[d - 1, j] + rcv_l[d, j]
             rs_l(d, j).start()
 
     def own_terms(d):
         values = chunk(ahead(d))
-        for j in range(4):
+        for j in range(SUBS):
             snd_r[d - 1, j] = part(values, j)
         values = chunk(ahead(Z - d))
-        for j in range(4):
+        for j in range(SUBS):
             snd_l[d - 1, j] = part(values, j)
 
     own_terms(2)
-    pass_on(3, (0, 1), (2, 3))
+    pass_on(3, FIRST, LAST)
     own_terms(1)
     values = chunk(z)
-    for j in range(4):
+    for j in range(SUBS):
         own[j] = part(values, j)
 
     feature_pair.wait_recv()
@@ -320,23 +343,23 @@
 
     def piece_copy(d):
         return remote(
-            F2.at[piece(lax.rem(chip + d, CHIPS))], f_recv.at[d - 1], fx_s.at[d - 1], fx_r.at[d - 1],
+            F2.at[piece(chip_at(d))], f_recv.at[d - 1], fx_s.at[d - 1], fx_r.at[d - 1],
             same_core(d),
         )
 
     for d in range(1, 5):
         piece_copy(d).start()
-    pass_on(2, (2, 3), (0, 1))
+    pass_on(2, LAST, FIRST)
     for d in range(5, 12):
         piece_copy(d).start()
-    pass_on(2, (0, 1), (2, 3))
+    pass_on(2, FIRST, LAST)
     for d in range(12, CHIPS):
         piece_copy(d).start()
-    pass_on(1, (2, 3), (0, 1))
+    pass_on(1, LAST, FIRST)
     for i in range(3):
         for d in range(1, Z):
             col_copy(i, d).wait_send()
-    pass_on(1, (0, 1), (2, 3))
+    pass_on(1, FIRST, LAST)
     for i in range(4):
         pair_copy(i).wait_send()
         for d in range(1, CHIPS):
@@ -359,14 +382,13 @@
         ag_r(1, j).start()
         ag_l(1, j).start()
 
-    for j in (2, 3):
+    for j in LAST:
         rs_r(1, j).wait_recv()
-    for j in (0, 1):
+    for j in FIRST:
         rs_l(1, j).wait_recv()
-    for j in (0, 1):
-        rs_r(1, j).wait_recv()
-        finish(j)
-    for j in (2, 3):
+    for i, j in zip(FIRST, LAST):
+        rs_r(1, i).wait_recv()
+        finish(i)
         rs_l(1, j).wait_recv()
         finish(j)
 
@@ -383,15 +405,15 @@
         return remote(fg.at[my_piece], fg.at[my_piece], fa_s.at[d - 1], fa_r.at[d - 1], same_core(d))
 
     def arrived_copy(d):
-        block = fg.at[piece(lax.rem(chip + CHIPS - d, CHIPS))]
+        block = fg.at[piece(chip_from(d))]
         return remote(block, block, fa_s.at[d - 1], fa_r.at[d - 1], same_core(d))
 
     def hand_copy(d):
-        block = fg.at[piece(lax.rem(chip + CHIPS - d, CHIPS))]
+        block = fg.at[piece(chip_from(d) if d else chip)]
         return remote(block, block, ff_s.at[d], ff_r.at[d], sibling)
 
     def hand_arrived(d):
-        start = (1 - core) * HALF + lax.rem(chip + CHIPS - d, CHIPS) * PIECE
+        start = (1 - core) * HALF + (chip_from(d) if d else chip) * PIECE
         block = fg.at[rows_at(start, PIECE, PIECE)]
         return remote(block, block, ff_s.at[d], ff_r.at[d], sibling)
 
@@ -409,25 +431,25 @@
 
     feature_pair.wait_send()
     for d in (1, 2):
-        for j in range(4):
+        for j in range(SUBS):
             arrived_r(d, j).wait_recv()
             ag_r(d + 1, j).start()
             arrived_l(d, j).wait_recv()
             ag_l(d + 1, j).start()
         for i in (4, 3) if d == 1 else (2, 1):
-            for j in range(4):
-                if i < 4 or j in (0, 1):
+            for j in range(SUBS):
+                if i < 4 or j in FIRST:
                     rs_r(i, j).wait_send()
-                if i < 4 or j in (2, 3):
+                if i < 4 or j in LAST:
                     rs_l(i, j).wait_send()
         if d == 1:
             for i in range(1, CHIPS):
                 piece_copy(i).wait_send()
-    for j in (0, 1):
+    for j in FIRST:
         arrived_r(3, j).wait_recv()
         ag_r(4, j).start()
         arrived_l(3, j).wait_recv()
-    for j in (2, 3):
+    for j in LAST:
         arrived_l(3, j).wait_recv()
         ag_l(4, j).start()
         arrived_r(3, j).wait_recv()
@@ -438,31 +460,34 @@
     for d in range(1, CHIPS):
         spread_copy(d).wait_send()
 
-    for j in (0, 1):
+    for j in FIRST:
         arrived_r(4, j).wait_recv()
-    for j in (2, 3):
+    for j in LAST:
         arrived_l(4, j).wait_recv()
 
     for d in range(CHIPS):
         hand_arrived(d).wait_recv()
 
     for d in (4, 3, 2, 1):
-        for j in range(4):
-            if d < 4 or j in (0, 1):
+        for j in range(SUBS):
+            if d < 4 or j in FIRST:
                 ag_r(d, j).wait_send()
-            if d < 4 or j in (2, 3):
+            if d < 4 or j in LAST:
                 ag_l(d, j).wait_send()
     for d in range(CHIPS):
         hand_copy(d).wait_send()
 
 
 def write_out(features, protos, features_out, protos_out, sems):
-    first = pltpu.make_async_copy(features, features_out, sems.at[0])
-    second = pltpu.make_async_copy(protos, protos_out, sems.at[1])
-    first.start()
-    second.start()
-    first.wait()
-    second.wait()
+    copies = []
+    for i in range(4):
+        for src, dst in ((features, features_out), (protos, protos_out)):
+            rows = pl.ds(i * (src.shape[0] // 4), src.shape[0] // 4)
+            copies.append(pltpu.make_async_copy(src.at[rows], dst.at[rows], sems.at[len(copies)]))
+    for copy in copies:
+        copy.start()
+    for copy in copies:
+        copy.wait()
 
 
 def on_device(student_features, teacher_features, student_protos, teacher_protos):
@@ -502,11 +527,11 @@
             vmem((4, 1, CROPS), F32),
             vmem((4, 1, CROPS), F32),
             vmem((4, CHIPS - 1, 1, CROPS), F32),
-            vmem((4, SUB, D), F32),
-            vmem((4, 4, SUB, D), F32),
-            vmem((4, 4, SUB, D), F32),
-            vmem((4, 4, SUB, D), F32),
-            vmem((4, 4, SUB, D), F32),
+            vmem((SUBS, SUB, D), F32),
+            vmem((4, SUBS, SUB, D), F32),
+            vmem((4, SUBS, SUB, D), F32),
+            vmem((4, SUBS, SUB, D), F32),
+            vmem((4, SUBS, SUB, D), F32),
             vmem((OWN, D), F32),
             vmem((OWN, 128), F32),
             vmem((HALF, D), F32),
@@ -519,7 +544,7 @@
             dma((4, CHIPS - 1)),
             dma((4, CHIPS - 1)),
         ]
-        + [dma((4, 4))] * 8
+        + [dma((4, SUBS))] * 8
         + [
             dma,
             dma,
@@ -542,7 +567,7 @@
         ),
         in_specs=[pl.BlockSpec(memory_space=pltpu.VMEM)] * 2,
         out_specs=[pl.BlockSpec(memory_space=pl.ANY)] * 2,
-        scratch_shapes=[dma((2,))],
+        scratch_shapes=[dma((8,))],
         compiler_params=pltpu.CompilerParams(vmem_limit_bytes=2 * 2**20),
     )(
         pltpu.with_memory_space_constraint(features, pltpu.VMEM),

time: 96.4 us -> 95.8 us (level)
  no operation moved by 1% of the time
where the time goes in v3:
time: 95.8 us
  Pallas kernels  95 us (99%)
    pallas_call x1, Pallas kernels, on_device(): pl.pallas_call(kernel, out_shape=(pltpu.VMEM((CROPS, D), F32), pltpu.VMEM...  93.1 us

profile of v3, /device:TPU:1, one launch (start us, length us, event | category | flops | bytes accessed | tf_op | source)
XLA Modules:
  0.0 95.8 jit_solution(11145518820586139273)
XLA Ops:
  0.6 93.1 %shard_map.59 = (f32[1536,256]{1,0:T(8,128)S(1)}, f32[2048,256]{1,0:T(8,128)S(1)}) custom-call(bf16[1536,256]{1,0:T(8,128)(2,1)} %sf_in.1, bf16[1536,256]{1,0:T(8,128)(2,1)} %tf_in.1, bf16[256,2048]{1,0:T(8,128)(2,1)} %sp_in.1, bf16[256,2048]{1,0:T(8,128)(2,1)} %tp_in.1), custom_call_target="tpu_custom_call" | custom-call | tf_op jit(solution)/shard_map/pallas_call | solution.py:496
  93.7 1.9 %shard_map.60 = (f32[1536,256]{1,0:T(8,128)}, f32[2048,256]{1,0:T(8,128)}) custom-call(f32[1536,256]{1,0:T(8,128)S(1)} %get-tuple-element.4.features, f32[2048,256]{1,0:T(8,128)S(1)} %get-tuple-element.5.protos), custom_call_target="tpu_custom_call" | custom-call | tf_op jit(solution)/shard_map/pallas_call | solution.py:562

commit v4 on v3

--- a/solution.py
+++ b/solution.py
@@ -44,25 +44,15 @@
 
 
 def normalise_rows(src, dst):
-    def body(i, carry):
-        rows = rows_at(i * 256, 256, 256)
-        floats = src[rows, :].astype(F32)
-        length = jnp.sqrt(jnp.sum(floats * floats, axis=1, keepdims=True) + epsilon)
-        dst[rows, :] = (floats / length).astype(BF16)
-        return carry
-
-    lax.fori_loop(0, CROPS // 256, body, 0)
+    floats = src[...].astype(F32)
+    length = jnp.sqrt(jnp.sum(floats * floats, axis=1, keepdims=True) + epsilon)
+    dst[...] = (floats / length).astype(BF16)
 
 
 def normalise_columns(src, dst):
-    def body(i, carry):
-        cols = rows_at(i * 256, 256, 256)
-        floats = src[:, cols].astype(F32)
-        length = jnp.sqrt(jnp.sum(floats * floats, axis=0, keepdims=True) + epsilon)
-        dst[:, cols] = (floats / length).astype(BF16)
-        return carry
-
-    lax.fori_loop(0, PROTOS // 256, body, 0)
+    floats = src[...].astype(F32)
+    length = jnp.sqrt(jnp.sum(floats * floats, axis=0, keepdims=True) + epsilon)
+    dst[...] = (floats / length).astype(BF16)
 
 
 def transpose_into(src, dst):
@@ -266,8 +256,12 @@
     to_rows(scale, col_scale)
     scale_rows(phT, col_scale, scaled_p)
     products(E, scaled_p, F2)
-    to_rows(grad_scale / row_total(2), row_scale)
-    scale_rows(sh, row_scale, scaled_s)
+    vector = grad_scale / row_total(2)
+    for i in range(CROPS // 128):
+        rows = slice(i * 128, (i + 1) * 128)
+        scale = jnp.broadcast_to(vector[:, rows], (128, 128)).T
+        row_scale[rows, :] = scale
+        scaled_s[rows, :] = (sh[rows, :].astype(F32) * wide(scale)).astype(BF16)
 
     def chunk(index):
         rows = rows_at(index * OWN, OWN, OWN)

time: 95.8 us -> 95.1 us (level)
  no operation moved by 1% of the time
where the time goes in v4:
time: 95.1 us; the launch traced here: 95 us
  Pallas kernels  94.2 us (99%)
    pallas_call x1, Pallas kernels, on_device(): pl.pallas_call(kernel, out_shape=(pltpu.VMEM((CROPS, D), F32), pltpu.VMEM...  92.3 us

profile of v4, /device:TPU:1, one launch (start us, length us, event | category | flops | bytes accessed | tf_op | source)
XLA Modules:
  0.0 95.0 jit_solution(153504620311160314)
XLA Ops:
  0.6 92.3 %shard_map.59 = (f32[1536,256]{1,0:T(8,128)S(1)}, f32[2048,256]{1,0:T(8,128)S(1)}) custom-call(bf16[1536,256]{1,0:T(8,128)(2,1)} %sf_in.1, bf16[1536,256]{1,0:T(8,128)(2,1)} %tf_in.1, bf16[256,2048]{1,0:T(8,128)(2,1)} %sp_in.1, bf16[256,2048]{1,0:T(8,128)(2,1)} %tp_in.1), custom_call_target="tpu_custom_call" | custom-call | tf_op jit(solution)/shard_map/pallas_call | solution.py:490
  93.0 1.9 %shard_map.60 = (f32[1536,256]{1,0:T(8,128)}, f32[2048,256]{1,0:T(8,128)}) custom-call(f32[1536,256]{1,0:T(8,128)S(1)} %get-tuple-element.4.features, f32[2048,256]{1,0:T(8,128)S(1)} %get-tuple-element.5.protos), custom_call_target="tpu_custom_call" | custom-call | tf_op jit(solution)/shard_map/pallas_call | solution.py:556
